TPU v7x, 256 devices: a whole 4x4x8 slice. The times are simulated.
256 devices in a mesh: region: 64 (over z, x, core), stream: 4 (over y).
Axes of the slice: x: 4, y: 4, z: 8, core: 2. Of those that a mesh axis runs over, the one named last changes fastest.
Arguments:
- crop_features: bfloat16 [512, 256, 2048], P(('region', 'stream')), may hold values from -6 to 6
- crop_counts: int32 [512], P(('region', 'stream')), may hold values from 1 to 256, 43690 in all
- bn_scale: float32 [2048], replicated, may hold values from 0.3 to 3
- bn_shift: float32 [2048], replicated, may hold values from -3 to 3
- projection: bfloat16 [2048, 512], replicated, may hold values from -0.125 to 0.125
- gallery: bfloat16 [512, 3, 32, 512], P(('region', 'stream')), may hold values from -6 to 6
- gallery_fill: int32 [512, 3], P(('region', 'stream')), may hold values from 1 to 32, 64 in all within a row
- adjacency: int32 [512, 128], P(('region', 'stream')), may hold values 0 or 1
Outputs:
- scores: float32 [512, 384, 256], P(('region', 'stream'))
Inputs may be any that keep to these rules, and one draw needn't show every extreme that they name: `crop_counts`: each camera has from 1 to 256 live crops; some camera has exactly 256. `gallery_fill`: each track has from 1 to 32 filled frames; every camera has a track with exactly 32.
All inputs are finite; a program needn't handle non-finite values. No bound on the sum of `crop_counts` or of `adjacency` on one device may be relied on, other than what follows from the above.
Results may differ from a plain program's by a relative error of at most 0.0024.
Values may be sent and summed in bfloat16 or wider, within the bound.
A program may use at most 128 MiB of HBM per device.

v0:
```python
import jax
import jax.numpy as jnp
from jax import lax
from jax.sharding import PartitionSpec as P


def embed_rows(feature_rows, bn_scale, bn_shift, projection):
    normed = (feature_rows.astype(jnp.float32) * bn_scale + bn_shift).astype(jnp.bfloat16)
    projected = jnp.dot(normed, projection, preferred_element_type=jnp.float32)
    return (
        projected * lax.rsqrt(jnp.sum(projected * projected, axis=-1, keepdims=True) + 1e-06)
    ).astype(jnp.bfloat16)


def frame_mask(fill_counts, frame_count):
    return jnp.arange(frame_count, dtype=jnp.int32)[None, None, :] < fill_counts[:, :, None]


def per_device(
    crop_features, crop_counts, bn_scale, bn_shift, projection, gallery, gallery_fill, adjacency
):
    cam_count, capacity, feat_width = crop_features.shape
    emb_width = projection.shape[1]
    track_count = gallery.shape[1]
    frame_count = gallery.shape[2]
    embeds = embed_rows(
        crop_features.reshape(cam_count * capacity, feat_width), bn_scale, bn_shift, projection
    ).reshape(cam_count, capacity, emb_width)
    piece_gallery = lax.all_gather(gallery, "region", axis=0, tiled=True)
    piece_fill = lax.all_gather(gallery_fill, "region", axis=0, tiled=True)
    similarity = jnp.einsum(
        "cpe,nkfe->cnkfp", embeds, piece_gallery, preferred_element_type=jnp.float32
    )
    piece_valid = frame_mask(piece_fill, frame_count)
    best_piece = jnp.max(jnp.where(piece_valid[None, :, :, :, None], similarity, -jnp.inf), axis=3)
    best_score = best_piece
    best_score = best_score.reshape(cam_count, -1, capacity)
    live_slots = jnp.arange(capacity, dtype=jnp.int32)[None, :] < crop_counts[:, None]
    adj_weight = jnp.repeat(adjacency, track_count, axis=1).astype(jnp.float32)
    return jnp.where(live_slots[:, None, :], best_score * adj_weight[:, :, None], 0.0)


def solution(mesh):
    return jax.shard_map(
        per_device,
        mesh=mesh,
        in_specs=(
            P(("region", "stream"), None, None),
            P(("region", "stream")),
            P(),
            P(),
            P(),
            P(("region", "stream"), None, None, None),
            P(("region", "stream"), None),
            P(("region", "stream"), None),
        ),
        out_specs=P(("region", "stream"), None, None),
        check_vma=False,
    )
```

profile of v0, /device:TPU:1, one launch (start us, length us, event | category | flops | bytes accessed | tf_op | source)
XLA Modules:
  0.0 138.7 jit_solution(16521374279310615268)
XLA Ops:
  6.5 0.0 copy-start
  6.5 0.0 all-gather.3.cloned.1.call-start
  6.5 0.7 all-gather.3.cloned.1.call-update
  7.3 48.2 %all-gather = s32[64,2,3]{2,1,0:T(2,128)S(1)} all-gather(s32[1,2,3]{2,1,0:T(2,128)} %bitcast.24), channel_id=1, replica_groups=mesh['region'=64,'stream'=4] {'region'}, dimensions={0}, use_global_device_ids=true | all-gather | bytes 1560 | tf_op jit(solution)/shard_map/all_gather | solution.py:30
  55.5 0.1 copy.15
  55.5 0.7 convert_element_type.27
  56.2 0.1 broadcast_in_dim.40
  56.3 0.2 convert_element_type.28
  56.5 0.1 copy.18
  56.7 0.7 iota_compare_fusion.1
  57.4 0.0 copy-done
  57.4 2.9 %multiply_reduce_fusion = (f32[512]{0:T(512)S(1)}, f32[512,512]{1,0:T(8,128)S(1)}) fusion(bf16[2048,512]{1,0:T(8,128)(2,1)S(1)} %copy-done, bf16[512,2048]{1,0:T(8,128)(2,1)} %bitcast.25, f32[2048]{0:T(1024)} %param.11, f32[2048]{0:T(1024)} %param.10), kind=kOutput, calls=%fused_computation.11 | convolution fusion | flops 1078459904 | bytes 5261312 | tf_op jit(solution)/shard_map/dot_general | solution.py:9
  60.4 0.1 multiply_convert_fusion
  60.5 43.8 %all-gather.3.cloned.1.call-done = bf16[128,3,32,512]{3,2,1,0:T(8,128)(2,1)} async-done(((bf16[2,3,32,512]{3,2,1,0:T(8,128)(2,1)}), bf16[128,3,32,512]{3,2,1,0:T(8,128)(2,1)}) %all-gather.3.cloned.1.call-update) | async-done | bytes 12582928 | tf_op jit(solution)/shard_map/all_gather | solution.py:29
  104.4 24.5 %select_reduce_fusion = f32[2,256,128,3]{2,1,3,0:T(8,128)} fusion(pred[128,3,32]{0,2,1:T(8,128)(4,1)S(1)} %iota_compare_fusion, bf16[2,256,512,1,1]{2,1,4,3,0:T(8,128)(2,1)S(1)} %bitcast.22, bf16[128,3,32,512]{3,2,1,0:T(8,128)(2,1)} %all-gather.3.cloned.1.call-done), kind=kOutput, calls=%fused_computation | convolution fusion | flops 6454837248 | bytes 13905920 | tf_op jit(solution)/shard_map/cpe,nkfe->cnkfp/dot_general | solution.py:31
  128.9 1.5 %copy.17 = f32[2,128,3,256]{3,0,2,1:T(2,128)S(1)} copy(f32[2,128,3,256]{1,3,2,0:T(8,128)} %bitcast.21) | data formatting | bytes 1572864 | tf_op jit(solution)/shard_map/reduce_max | solution.py:35
  130.4 0.5 fusion.11
  130.9 0.9 copy.19
  (2 shorter events, 0.0 us)
Async XLA Ops:
  6.5 50.9 %copy-start = (bf16[2048,512]{1,0:T(8,128)(2,1)S(1)}, bf16[2048,512]{1,0:T(8,128)(2,1)}, u32[]{:S(2)}) copy-start(bf16[2048,512]{1,0:T(8,128)(2,1)} %param.12) | copy-start | bytes 6291460
  6.5 97.8 %all-gather.3.cloned.1.call-start = ((), (), s32[]{:S(2)}) async-start(), calls=%async_computation | async-start | bytes 12779520 | tf_op jit(solution)/shard_map/all_gather | solution.py:29
Sparse Core Ops, SparseCore 0:
  10.1 94.2 all-gather.2
where the time goes:
time: 139 us
  blocking collectives  48.2 us (35%)
  waiting for transfers between devices  44.5 us (32%)
  matrix products  27.4 us (20%)
  between operations  13.4 us (10%)
  local copies, waits for them, and re-layouts  3 us (2%)
  other arithmetic  2.12 us (2%)
    all_gather x1, blocking collectives, per_device(): piece_fill = lax.all_gather(gallery_fill, 'region', axis=0, tiled=True)  48.2 us
    all_gather x1, waiting for transfers between devices, per_device(): piece_gallery = lax.all_gather(gallery, 'region', axis=0, tiled=True)  43.8 us
    dot_general x1, matrix products, per_device(): jnp.einsum('cpe,nkfe->cnkfp', embeds, piece_gallery, preferred_element_ty...  24.5 us
    dot_general x1, matrix products, embed_rows(): projected = jnp.dot(normed, projection, preferred_element_type=jnp.float32)  2.94 us
  transfers between devices with their start and end apart: 1, of which 1 were waited for; matrix products, arithmetic and copies ran while one was open for 4% of the time, Pallas kernels for 0%

commit v1 on v0

v1 whole, which is shorter than its diff:
```python
import functools

import jax
import jax.numpy as jnp
from jax import lax
from jax.experimental import pallas as pl
from jax.experimental.pallas import tpu as pltpu
from jax.sharding import PartitionSpec as P

MESH = pl.DeviceIdType.MESH
CAMS, CROPS, FEAT, EMB = 2, 256, 2048, 512
TRACKS, FRAMES, KEPT, HALF = 3, 32, 64, 32
NZ, ROWS, NEIGH = 8, 12, 128


def kernel(
    feat, counts, scale, shift, proj, gall, fill, adj, out,
    fv, pv, gv, sc, sh, av, adjc, normed, gal, meta, emb, ro, rss, rsr, rps, rpr,
    lsem, zs, zr, zms, zmr, xs, xr, es, er, ss, sr, ps, pr,
):
    r, s = lax.axis_index("region"), lax.axis_index("stream")
    z, x, c = r // 8, (r // 2) % 4, r % 2
    xi = x % 2
    sib = (r + 1 - 2 * c, s)
    xm = (z * 8 + (x + 1 - 2 * xi) * 2 + c, s)
    pm = (z * 8 + (3 - x) * 2 + c, s)
    pmo = (z * 8 + (3 - x) * 2 + 1 - c, s)
    zp = (((z + 1) % NZ) * 8 + x * 2 + c, s)
    zn = (((z + NZ - 1) % NZ) * 8 + x * 2 + c, s)

    def at(d):
        return (z + d + NZ) % NZ

    local = [
        pltpu.make_async_copy(gall, gv, lsem.at[0]),
        pltpu.make_async_copy(scale, sc, lsem.at[1]),
        pltpu.make_async_copy(shift, sh, lsem.at[2]),
        pltpu.make_async_copy(proj, pv, lsem.at[3]),
        pltpu.make_async_copy(feat.at[0], fv.at[0], lsem.at[4]),
        pltpu.make_async_copy(feat.at[1], fv.at[1], lsem.at[5]),
        pltpu.make_async_copy(adj, av, lsem.at[6]),
    ]
    for cp in local:
        cp.start()
    barrier = pltpu.get_barrier_semaphore()
    peers = (sib, xm, pm, pmo, zp, zn)
    for t in peers:
        pl.semaphore_signal(barrier, inc=1, device_id=t, device_id_type=MESH)

    local[0].wait()
    row = lax.broadcasted_iota(jnp.int32, (KEPT, TRACKS * FRAMES), 0)
    src = lax.broadcasted_iota(jnp.int32, (KEPT, TRACKS * FRAMES), 1)
    notes = []
    for cam in range(CAMS):
        f0, f1 = fill[cam, 0], fill[cam, 1]
        full = jnp.where(f0 == FRAMES, 0, jnp.where(f1 == FRAMES, 1, 2))
        first = jnp.where(full == 0, 1, 0)
        second = jnp.where(full == 2, 1, 2)
        cut = jnp.where(full == 0, f1, f0)
        notes += [cut, full]
        want = jnp.where(
            row < HALF,
            full * FRAMES + row,
            jnp.where(row - HALF < cut, first * FRAMES + row - HALF, second * FRAMES + row - HALF - cut),
        )
        pick = (src == want).astype(jnp.float32).astype(jnp.bfloat16)
        kept = jnp.dot(pick, gv[cam].reshape(TRACKS * FRAMES, EMB), preferred_element_type=jnp.float32)
        gal[z, xi, cam] = kept.astype(jnp.bfloat16)
    line = lax.broadcasted_iota(jnp.int32, (8, 128), 0)
    meta[z, xi] = jnp.where(
        line == 0, notes[0], jnp.where(line == 1, notes[2], jnp.where(line == 2, notes[1], notes[3]))
    )
    pl.semaphore_wait(barrier, len(peers))

    sent = []

    def send(ref_from, ref_to, s_sem, r_sem, to):
        cp = pltpu.make_async_remote_copy(
            src_ref=ref_from, dst_ref=ref_to, send_sem=s_sem, recv_sem=r_sem, device_id=to, device_id_type=MESH
        )
        cp.start()
        sent.append(cp)

    def arrive(ref, s_sem, r_sem):
        pltpu.make_async_remote_copy(
            src_ref=ref, dst_ref=ref, send_sem=s_sem, recv_sem=r_sem, device_id=sib, device_id_type=MESH
        ).wait_recv()

    def unit(stream, zz, part):
        ref = gal.at[zz, 1 - xi if stream == 1 else xi, 1 if stream == 2 else 0]
        return ref if part is None else ref.at[pl.ds(part * HALF, HALF)]

    def note(stream, zz):
        return meta.at[zz, 1 - xi if stream == 1 else xi]

    def z_send(stream, way, hop):
        zz = at(-(hop - 1) if way == 0 else hop - 1)
        ref = unit(stream, zz, way if hop == 4 else None)
        to = zp if way == 0 else zn
        send(ref, ref, zs.at[way, stream, hop - 1], zr.at[way, stream, hop - 1], to)
        if stream < 2 and not (way == 1 and hop == 4):
            ref = note(stream, zz)
            send(ref, ref, zms.at[way, stream, hop - 1], zmr.at[way, stream, hop - 1], to)

    def x_ref(cam, d, part):
        ref = gal.at[at(d), xi, cam]
        return ref if part is None else ref.at[pl.ds(part * HALF, HALF)]

    def x_index(hop, way):
        return 1 if hop == 0 else 2 + (hop - 1) * 2 + way

    def x_send(cam, hop, way):
        k = 0 if cam == 0 else x_index(hop, way)
        ref = x_ref(cam, -hop if way == 0 else hop, way if hop == 4 else None)
        send(ref, ref, xs.at[k], xr.at[k], xm)
        if cam == 0:
            send(meta.at[z, xi], meta.at[z, xi], xs.at[10], xr.at[10], xm)

    def x_arrive(cam, hop, way):
        k = 0 if cam == 0 else x_index(hop, way)
        ref = gal.at[at(-hop if way == 0 else hop), 1 - xi, cam]
        if hop == 4:
            ref = ref.at[pl.ds(way * HALF, HALF)]
        arrive(ref, xs.at[k], xr.at[k])
        if cam == 0:
            arrive(meta.at[z, 1 - xi], xs.at[10], xr.at[10])

    def z_arrive(stream, hop):
        for way in range(2):
            zz = at(-hop if way == 0 else hop)
            arrive(unit(stream, zz, way if hop == 4 else None), zs.at[way, stream, hop - 1], zr.at[way, stream, hop - 1])
            if stream < 2 and not (way == 1 and hop == 4):
                arrive(note(stream, zz), zms.at[way, stream, hop - 1], zmr.at[way, stream, hop - 1])
            if hop < 4:
                z_send(stream, way, hop + 1)
            if stream == 2:
                x_send(1, hop, way)

    z_send(2, 0, 1)
    z_send(2, 1, 1)
    x_send(0, 0, 0)
    z_send(0, 0, 1)
    z_send(0, 1, 1)
    x_send(1, 0, 0)

    def embed(cam):
        rows = fv[cam].astype(jnp.float32) * sc[...].reshape(1, FEAT) + sh[...].reshape(1, FEAT)
        normed[...] = rows.astype(jnp.bfloat16)
        projected = jnp.dot(normed[...], pv[...], preferred_element_type=jnp.float32)
        total = jnp.sum(projected * projected, axis=-1, keepdims=True)
        unit_rows = (projected * lax.rsqrt(total + 1e-06)).astype(jnp.bfloat16)
        emb[0, cam] = unit_rows.T
        send(emb.at[0, cam], emb.at[2, cam], es.at[0, cam], er.at[0, cam], pm)
        send(emb.at[0, cam], emb.at[1, cam], es.at[1, cam], er.at[1, cam], sib)

    local[1].wait()
    local[2].wait()
    local[3].wait()
    local[4].wait()
    embed(0)
    x_arrive(0, 0, 0)
    z_send(1, 0, 1)
    z_send(1, 1, 1)
    local[5].wait()
    embed(1)

    def emb_arrive(grp, cam):
        k = {2: 0, 1: 1, 3: 2}[grp]
        arrive(emb.at[grp, cam], es.at[k, cam], er.at[k, cam])
        if grp == 2:
            send(emb.at[2, cam], emb.at[3, cam], es.at[2, cam], er.at[2, cam], sib)

    def score(zz, grp, cam):
        sims = jnp.dot(
            gal[zz].reshape(4 * KEPT, EMB), emb[grp, cam], preferred_element_type=jnp.float32
        )
        frame = lax.broadcasted_iota(jnp.int32, (HALF, CROPS), 0)
        rows = []
        for q in range(4):
            cut = meta[zz, q // 2, pl.ds(q % 2, 1), :]
            full = meta[zz, q // 2, pl.ds(2 + q % 2, 1), :]
            cut = jnp.concatenate([cut, cut], axis=1)
            full = jnp.concatenate([full, full], axis=1)
            whole = sims[q * KEPT : q * KEPT + HALF]
            mixed = sims[q * KEPT + HALF : (q + 1) * KEPT]
            mine = frame < cut
            a = jnp.max(whole, axis=0, keepdims=True)
            u = jnp.max(jnp.where(mine, mixed, -jnp.inf), axis=0, keepdims=True)
            v = jnp.max(jnp.where(mine, -jnp.inf, mixed), axis=0, keepdims=True)
            rows.append(jnp.where(full == 0, a, u))
            rows.append(jnp.where(full == 1, a, jnp.where(full == 0, u, v)))
            rows.append(jnp.where(full == 2, a, v))
        rows.append(jnp.zeros((4, CROPS), jnp.float32))
        return jnp.concatenate(rows, axis=0)

    def work(hop, grp, cam):
        ways = 1 if hop in (0, 4) else 2

        def body(i, carry):
            zz = at(hop - 2 * hop * i)
            got = score(zz, grp, cam)
            if grp == 0:
                ro[zz, cam] = got
            elif grp == 1:
                rss[zz, cam] = got
            else:
                rps[grp - 2, zz, cam] = got.astype(jnp.bfloat16)
            return carry

        lax.fori_loop(0, ways, body, 0)

    def offsets(hop):
        return ((0, hop),) if hop in (0, 4) else ((0, hop), (1, -hop))

    def give_sib(hop):
        for i, d in offsets(hop):
            k = hop * 2 + i
            send(rss.at[at(d)], rsr.at[at(d)], ss.at[k], sr.at[k], sib)

    def give_pair(hop):
        for t, to in enumerate((pm, pmo)):
            for i, d in offsets(hop):
                k = hop * 2 + i
                send(rps.at[t, at(d)], rpr.at[t, at(d)], ps.at[t, k], pr.at[t, k], to)

    local[6].wait()
    n_row = lax.broadcasted_iota(jnp.int32, (NEIGH * TRACKS, NEIGH), 0)
    n_col = lax.broadcasted_iota(jnp.int32, (NEIGH * TRACKS, NEIGH), 1) * TRACKS
    same = (n_row >= n_col) & (n_row < n_col + TRACKS)
    for cam in range(CAMS):
        spread = jnp.where(same, av[pl.ds(cam, 1), :].astype(jnp.float32), 0.0).astype(jnp.bfloat16)
        adjc[cam] = jnp.dot(spread, jnp.ones((NEIGH, 128), jnp.bfloat16), preferred_element_type=jnp.float32)

    z_arrive(2, 1)
    z_arrive(0, 1)
    x_arrive(1, 0, 0)
    emb_arrive(1, 0)
    emb_arrive(1, 1)
    work(0, 0, 0)
    work(0, 0, 1)
    z_arrive(1, 1)
    work(0, 1, 0)
    work(0, 1, 1)
    give_sib(0)
    x_arrive(1, 1, 0)
    x_arrive(1, 1, 1)
    work(1, 0, 0)
    work(1, 0, 1)
    z_arrive(2, 2)
    work(1, 1, 0)
    work(1, 1, 1)
    give_sib(1)
    z_arrive(0, 2)
    emb_arrive(2, 0)
    z_arrive(1, 2)
    x_arrive(1, 2, 0)
    x_arrive(1, 2, 1)
    work(2, 0, 0)
    work(2, 0, 1)
    z_arrive(2, 3)
    emb_arrive(3, 0)
    work(2, 1, 0)
    work(2, 1, 1)
    give_sib(2)
    work(0, 2, 0)
    work(0, 3, 0)
    z_arrive(0, 3)
    work(1, 2, 0)
    work(1, 3, 0)
    work(2, 2, 0)
    work(2, 3, 0)
    z_arrive(1, 3)
    x_arrive(1, 3, 0)
    x_arrive(1, 3, 1)
    work(3, 0, 0)
    work(3, 0, 1)
    emb_arrive(2, 1)
    z_arrive(2, 4)
    work(3, 1, 0)
    work(3, 1, 1)
    give_sib(3)
    emb_arrive(3, 1)
    for hop in range(3):
        work(hop, 2, 1)
        work(hop, 3, 1)
        give_pair(hop)
    z_arrive(0, 4)
    z_arrive(1, 4)
    for cam in range(CAMS):
        work(3, 2, cam)
        work(3, 3, cam)
    give_pair(3)
    x_arrive(1, 4, 0)
    x_arrive(1, 4, 1)
    for cam in range(CAMS):
        work(4, 2, cam)
        work(4, 3, cam)
    give_pair(4)
    for cam in range(CAMS):
        work(4, 1, cam)
    give_sib(4)
    for cam in range(CAMS):
        work(4, 0, cam)

    lane = lax.broadcasted_iota(jnp.int32, (24, CROPS), 1)

    def weave(even, odd):
        return jnp.concatenate([even[0:6], odd[0:6], even[6:12], odd[6:12]], axis=0)

    def finish(hop):
        for i, d in offsets(hop):
            k = hop * 2 + i
            arrive(rsr.at[at(d)], ss.at[k], sr.at[k])
            for t in range(2):
                arrive(rpr.at[t, at(d)], ps.at[t, k], pr.at[t, k])

        def body(i, carry):
            zz = at(hop - 2 * hop * i)
            for cam in range(CAMS):
                for side in range(2):
                    if side == 0:
                        here, there = ro[zz, cam], rsr[zz, cam]
                    else:
                        here, there = rpr[0, zz, cam].astype(jnp.float32), rpr[1, zz, cam].astype(jnp.float32)
                    block = weave(jnp.where(c == 0, here, there), jnp.where(c == 0, there, here))
                    cls = x // 2 if side == 0 else 1 - x // 2
                    at_row = pl.multiple_of(zz * 48 + cls * 24, 8)
                    factor = adjc[cam, pl.ds(at_row, 24), :]
                    block = block * jnp.concatenate([factor, factor], axis=1)
                    out[cam, pl.ds(at_row, 24), :] = jnp.where(lane < counts[cam], block, 0.0)
            return carry

        lax.fori_loop(0, 1 if hop in (0, 4) else 2, body, 0)

    for hop in range(5):
        finish(hop)
    for cp in sent:
        cp.wait_send()


def per_device(feat, counts, scale, shift, proj, gall, fill, adj):
    hbm = pl.BlockSpec(memory_space=pl.ANY)
    smem = pl.BlockSpec(memory_space=pltpu.SMEM)
    vmem = pl.BlockSpec(memory_space=pltpu.VMEM)
    bf, f32, dma = jnp.bfloat16, jnp.float32, pltpu.SemaphoreType.DMA
    return pl.pallas_call(
        kernel,
        name="match",
        out_shape=jax.ShapeDtypeStruct((CAMS, NEIGH * TRACKS, CROPS), f32),
        in_specs=[hbm, smem, hbm, hbm, hbm, hbm, smem, hbm],
        out_specs=vmem,
        scratch_shapes=[
            pltpu.VMEM((CAMS, CROPS, FEAT), bf),
            pltpu.VMEM((FEAT, EMB), bf),
            pltpu.VMEM((CAMS, TRACKS, FRAMES, EMB), bf),
            pltpu.VMEM((FEAT,), f32),
            pltpu.VMEM((FEAT,), f32),
            pltpu.VMEM((CAMS, NEIGH), jnp.int32),
            pltpu.VMEM((CAMS, NEIGH * TRACKS, 128), f32),
            pltpu.VMEM((CROPS, FEAT), bf),
            pltpu.VMEM((NZ, 2, CAMS, KEPT, EMB), bf),
            pltpu.VMEM((NZ, 2, 8, 128), jnp.int32),
            pltpu.VMEM((4, CAMS, EMB, CROPS), bf),
            pltpu.VMEM((NZ, CAMS, 16, CROPS), f32),
            pltpu.VMEM((NZ, CAMS, 16, CROPS), f32),
            pltpu.VMEM((NZ, CAMS, 16, CROPS), f32),
            pltpu.VMEM((2, NZ, CAMS, 16, CROPS), bf),
            pltpu.VMEM((2, NZ, CAMS, 16, CROPS), bf),
            dma((7,)),
            dma((2, 3, 4)),
            dma((2, 3, 4)),
            dma((2, 2, 4)),
            dma((2, 2, 4)),
            dma((11,)),
            dma((11,)),
            dma((3, CAMS)),
            dma((3, CAMS)),
            dma((10,)),
            dma((10,)),
            dma((2, 10)),
            dma((2, 10)),
        ],
        compiler_params=pltpu.CompilerParams(
            collective_id=0, has_side_effects=True, vmem_limit_bytes=40 * 2**20
        ),
    )(feat, counts, scale, shift, proj, gall, fill, adj)


def solution(mesh):
    return jax.shard_map(
        per_device,
        mesh=mesh,
        in_specs=(
            P(("region", "stream"), None, None),
            P(("region", "stream")),
            P(),
            P(),
            P(),
            P(("region", "stream"), None, None, None),
            P(("region", "stream"), None),
            P(("region", "stream"), None),
        ),
        out_specs=P(("region", "stream"), None, None),
        check_vma=False,
    )
```

time: 139 us -> 49.8 us (0.36)
  blocking collectives: 48.2 us -> 0 us
  waiting for transfers between devices: 44.5 us -> 0 us
  Pallas kernels: 0 us -> 41.1 us
  matrix products: 27.4 us -> 0 us
  between operations: 13.4 us -> 0.02 us
  local copies, waits for them, and re-layouts: 3 us -> 8.39 us
  other arithmetic: 2.12 us -> 0 us
    all_gather x1 -> x0, blocking collectives: 48.2 us -> none  [per_device(): piece_fill = lax.all_gather(gallery_fill, 'region', axis=0, tiled=True)]
    all_gather x1 -> x0, waiting for transfers between devices: 43.8 us -> none  [per_device(): piece_gallery = lax.all_gather(gallery, 'region', axis=0, tiled=True)]
    pallas_call x0 -> x1, Pallas kernels: none -> 41.1 us  [per_device(): pl.pallas_call(kernel, name='match', out_shape=jax.ShapeDtypeStruct((CAMS...]
    dot_general x2 -> x0, matrix products: 27.4 us -> none  [the longest x1 24.5 us: per_device(): jnp.einsum('cpe,nkfe->cnkfp', embeds, piece_gallery, preferred_element_ty...]
    unnamed x3 -> x17, local copies, waits for them, and re-layouts: 0.06 us -> 8.39 us
    reduce_max x1 -> x0, local copies, waits for them, and re-layouts: 1.55 us -> none  [per_device(): jnp.max(jnp.where(piece_valid[None, :, :, :, None], similarity, -jnp.inf)...]
  transfers between devices with their start and end apart: 1 -> 0, of which waited for: 1 -> 0; matrix products, arithmetic and copies ran while one was open for 4% -> 0% of each run, Pallas kernels for 0% -> 0%
where the time goes in v1:
time: 49.8 us; the launch traced here: 49.5 us
  Pallas kernels  41.1 us (83%)
  local copies, waits for them, and re-layouts  8.39 us (17%)
    pallas_call x1, Pallas kernels, per_device(): pl.pallas_call(kernel, name='match', out_shape=jax.ShapeDtypeStruct((CAMS...  41.1 us
    unnamed x17, local copies, waits for them, and re-layouts  8.39 us

profile of v1, /device:TPU:1, one launch (start us, length us, event | category | flops | bytes accessed | tf_op | source)
XLA Modules:
  0.0 49.5 jit_solution(3382637815312927023)
XLA Ops:
  0.0 0.0 copy-start
  0.0 1.6 %copy-done = bf16[2,256,2048]{2,1,0:T(8,128)(2,1)S(1)} copy-done((bf16[2,256,2048]{2,1,0:T(8,128)(2,1)S(1)}, bf16[2,256,2048]{2,1,0:T(8,128)(2,1)}, u32[]{:S(2)}) %copy-start) | copy-done | bytes 2097176
  1.6 0.0 copy-start.1
  1.6 1.6 %copy-done.1 = bf16[2048,512]{1,0:T(8,128)(2,1)S(1)} copy-done((bf16[2048,512]{1,0:T(8,128)(2,1)S(1)}, bf16[2048,512]{1,0:T(8,128)(2,1)}, u32[]{:S(2)}) %copy-start.1) | copy-done | bytes 2097176
  3.2 0.0 copy-start.2
  3.2 0.9 %copy-done.2 = bf16[2,3,32,512]{3,2,1,0:T(8,128)(2,1)S(1)} copy-done((bf16[2,3,32,512]{3,2,1,0:T(8,128)(2,1)S(1)}, bf16[2,3,32,512]{3,2,1,0:T(8,128)(2,1)}, u32[]{:S(2)}) %copy-start.2) | copy-done | bytes 196632
  4.1 0.0 copy-start.3
  4.1 0.7 %copy-done.3 = f32[2048]{0:T(1024)S(1)} copy-done((f32[2048]{0:T(1024)S(1)}, f32[2048]{0:T(1024)}, u32[]{:S(2)}) %copy-start.3) | copy-done | bytes 8216
  4.8 0.0 copy-start.4
  4.8 0.7 %copy-done.4 = f32[2048]{0:T(1024)S(1)} copy-done((f32[2048]{0:T(1024)S(1)}, f32[2048]{0:T(1024)}, u32[]{:S(2)}) %copy-start.4) | copy-done | bytes 8216
  5.5 0.0 copy-start.5
  5.5 0.7 %copy-done.5 = s32[2,3]{1,0:T(2,128)S(1)} copy-done((s32[2,3]{1,0:T(2,128)S(1)}, s32[2,3]{1,0:T(2,128)}, u32[]{:S(2)}) %copy-start.5) | copy-done | bytes 48
  6.2 0.0 copy-start.6
  6.2 0.7 %copy-done.6 = s32[2,128]{1,0:T(2,128)S(1)} copy-done((s32[2,128]{1,0:T(2,128)S(1)}, s32[2,128]{1,0:T(2,128)}, u32[]{:S(2)}) %copy-start.6) | copy-done | bytes 1048
  6.9 0.0 copy-start.7
  6.9 0.7 %copy-done.7 = s32[2]{0:T(128)S(1)} copy-done((s32[2]{0:T(128)S(1)}, s32[2]{0:T(128)}, u32[]{:S(2)}) %copy-start.7) | copy-done | bytes 32
  7.5 41.1 %match.1 = f32[2,384,256]{2,1,0:T(8,128)S(1)} custom-call(bf16[2,256,2048]{2,1,0:T(8,128)(2,1)S(1)} %copy-done, s32[2]{0:T(128)S(1)} %copy-done.7, f32[2048]{0:T(1024)S(1)} %copy-done.3, f32[2048]{0:T(1024)S(1)} %copy-done.4, bf16[2048,512]{1,0:T(8,128)(2,1)S(1)} %copy-done.1, bf16[2,3,32,512]{3,2,1,0:T(8,128)(2,1)S(1)} %copy-done.2, s32[2,3]{1,0:T(2,128)S(1)} %copy-done.5, ...), custom_call_target="tpu_custom_call" | custom-call | tf_op jit(solution)/shard_map/match/pallas_call | solution.py:346
  48.6 0.9 %copy.10 = f32[2,384,256]{2,1,0:T(8,128)} copy(f32[2,384,256]{2,1,0:T(8,128)S(1)} %match.1) | data formatting | bytes 1572864
Async XLA Ops:
  0.0 1.6 %copy-start = (bf16[2,256,2048]{2,1,0:T(8,128)(2,1)S(1)}, bf16[2,256,2048]{2,1,0:T(8,128)(2,1)}, u32[]{:S(2)}) copy-start(bf16[2,256,2048]{2,1,0:T(8,128)(2,1)} %feat.1) | copy-start | bytes 6291460
  1.6 1.6 %copy-start.1 = (bf16[2048,512]{1,0:T(8,128)(2,1)S(1)}, bf16[2048,512]{1,0:T(8,128)(2,1)}, u32[]{:S(2)}) copy-start(bf16[2048,512]{1,0:T(8,128)(2,1)} %proj.1) | copy-start | bytes 6291460
  3.2 0.9 %copy-start.2 = (bf16[2,3,32,512]{3,2,1,0:T(8,128)(2,1)S(1)}, bf16[2,3,32,512]{3,2,1,0:T(8,128)(2,1)}, u32[]{:S(2)}) copy-start(bf16[2,3,32,512]{3,2,1,0:T(8,128)(2,1)} %gall.1) | copy-start | bytes 589828
  4.1 0.7 %copy-start.3 = (f32[2048]{0:T(1024)S(1)}, f32[2048]{0:T(1024)}, u32[]{:S(2)}) copy-start(f32[2048]{0:T(1024)} %scale.1) | copy-start | bytes 24580
  4.8 0.7 %copy-start.4 = (f32[2048]{0:T(1024)S(1)}, f32[2048]{0:T(1024)}, u32[]{:S(2)}) copy-start(f32[2048]{0:T(1024)} %shift.1) | copy-start | bytes 24580
  5.5 0.7 %copy-start.5 = (s32[2,3]{1,0:T(2,128)S(1)}, s32[2,3]{1,0:T(2,128)}, u32[]{:S(2)}) copy-start(s32[2,3]{1,0:T(2,128)} %fill.1) | copy-start | bytes 76
  6.2 0.7 %copy-start.6 = (s32[2,128]{1,0:T(2,128)S(1)}, s32[2,128]{1,0:T(2,128)}, u32[]{:S(2)}) copy-start(s32[2,128]{1,0:T(2,128)} %adj.1) | copy-start | bytes 3076
  6.9 0.7 %copy-start.7 = (s32[2]{0:T(128)S(1)}, s32[2]{0:T(128)}, u32[]{:S(2)}) copy-start(s32[2]{0:T(128)} %counts.1) | copy-start | bytes 28

commit v2 on v1

v2 whole, which is shorter than its diff:
```python
import functools

import jax
import jax.numpy as jnp
from jax import lax
from jax.experimental import pallas as pl
from jax.experimental.pallas import tpu as pltpu
from jax.sharding import PartitionSpec as P

MESH = pl.DeviceIdType.MESH
CAMS, CROPS, FEAT, EMB = 2, 256, 2048, 512
TRACKS, FRAMES, KEPT, HALF = 3, 32, 64, 32
NZ, ROWS, NEIGH = 8, 12, 128
DELTA = (0, 1, -1, 2, -2, 3, -3, 4)
SIB_PARTS = ((0, 4), (4, 2), (6, 2))
MESSAGES = (
    ((0, 0), (1, 0), (2, 0), (3, 0)),
    ((0, 1), (1, 1), (2, 1), (3, 1)),
    ((4, 0), (4, 1), (5, 0), (5, 1)),
    ((6, 0), (6, 1), (7, 0), (7, 1)),
)
PLACE = {p: (m, j) for m, part in enumerate(MESSAGES) for j, p in enumerate(part)}


def kernel(
    feat, scale, shift, proj, gall, fill_in, adj, out,
    fill, fv, pv, gv, sc, sh, av, adjc, normed, gal, meta, emb, res, rsr, rps, rpr, outv,
    lsem, zs, zr, ms, mr, xs, xr, es, er, ss, sr, ps, pr, osem,
):
    r, s = lax.axis_index("region"), lax.axis_index("stream")
    z, x, c = r // 8, (r // 2) % 4, r % 2
    xi = x % 2

    def device(z2, x2, c2):
        return (z2 * 8 + x2 * 2 + c2, s)

    sib = device(z, x, 1 - c)
    xm = device(z, x + 1 - 2 * xi, c)
    pm = device(z, 3 - x, c)
    pmo = device(z, 3 - x, 1 - c)
    zp = device((z + 1) % NZ, x, c)
    zn = device((z + NZ - 1) % NZ, x, c)

    def at(d):
        return (z + d + NZ) % NZ

    local = [
        pltpu.make_async_copy(gall, gv, lsem.at[0]),
        pltpu.make_async_copy(fill_in, fill, lsem.at[7]),
        pltpu.make_async_copy(scale, sc, lsem.at[1]),
        pltpu.make_async_copy(shift, sh, lsem.at[2]),
        pltpu.make_async_copy(proj, pv, lsem.at[3]),
        pltpu.make_async_copy(feat.at[0], fv.at[0], lsem.at[4]),
        pltpu.make_async_copy(feat.at[1], fv.at[1], lsem.at[5]),
        pltpu.make_async_copy(adj, av, lsem.at[6]),
    ]
    for cp in local:
        cp.start()
    barrier = pltpu.get_barrier_semaphore()
    peers = (sib, xm, pm, pmo, zp, zn)
    for t in peers:
        pl.semaphore_signal(barrier, inc=1, device_id=t, device_id_type=MESH)

    local[0].wait()
    local[1].wait()
    row = lax.broadcasted_iota(jnp.int32, (KEPT, TRACKS * FRAMES), 0)
    src = lax.broadcasted_iota(jnp.int32, (KEPT, TRACKS * FRAMES), 1)
    notes = []
    for cam in range(CAMS):
        f0, f1 = fill[cam, 0], fill[cam, 1]
        full = jnp.where(f0 == FRAMES, 0, jnp.where(f1 == FRAMES, 1, 2))
        first = jnp.where(full == 0, 1, 0)
        second = jnp.where(full == 2, 1, 2)
        cut = jnp.where(full == 0, f1, f0)
        notes += [cut, full]
        want = jnp.where(
            row < HALF,
            full * FRAMES + row,
            jnp.where(row - HALF < cut, first * FRAMES + row - HALF, second * FRAMES + row - HALF - cut),
        )
        pick = (src == want).astype(jnp.float32).astype(jnp.bfloat16)
        kept = jnp.dot(pick, gv[cam].reshape(TRACKS * FRAMES, EMB), preferred_element_type=jnp.float32)
        gal[z, xi, cam] = kept.astype(jnp.bfloat16)
    line = lax.broadcasted_iota(jnp.int32, (8, 128), 0)
    meta[z, xi] = jnp.where(
        line == 0, notes[0], jnp.where(line == 1, notes[2], jnp.where(line == 2, notes[1], notes[3]))
    )
    pl.semaphore_wait(barrier, len(peers))

    sent = []

    def send(ref_from, ref_to, s_sem, r_sem, to):
        cp = pltpu.make_async_remote_copy(
            src_ref=ref_from, dst_ref=ref_to, send_sem=s_sem, recv_sem=r_sem, device_id=to, device_id_type=MESH
        )
        cp.start()
        sent.append(cp)

    def drain(keep):
        while len(sent) > keep:
            sent.pop(0).wait_send()

    def arrive(ref, s_sem, r_sem):
        pltpu.make_async_remote_copy(
            src_ref=ref, dst_ref=ref, send_sem=s_sem, recv_sem=r_sem, device_id=sib, device_id_type=MESH
        ).wait_recv()

    def unit(stream, zz, part):
        ref = gal.at[zz, 1 - xi if stream == 1 else xi, 1 if stream == 2 else 0]
        return ref if part is None else ref.at[pl.ds(part * HALF, HALF)]

    def note(stream, zz):
        return meta.at[zz, 1 - xi if stream == 1 else xi]

    def noted(stream, way, hop):
        return stream < 2 and not (way == 1 and hop == 4)

    def z_send(stream, way, hop):
        ref = unit(stream, at(-(hop - 1) if way == 0 else hop - 1), way if hop == 4 else None)
        to = zp if way == 0 else zn
        send(ref, ref, zs.at[way, stream, hop - 1], zr.at[way, stream, hop - 1], to)
        if noted(stream, way, hop):
            ref = note(stream, at(-(hop - 1) if way == 0 else hop - 1))
            send(ref, ref, ms.at[way, stream, hop - 1], mr.at[way, stream, hop - 1], to)

    def x_unit(column, cam, hop, way):
        ref = gal.at[at(-hop if way == 0 else hop), column, cam]
        return ref.at[pl.ds(way * HALF, HALF)] if hop == 4 else ref

    def x_index(cam, hop, way):
        return 0 if cam == 0 else 1 if hop == 0 else 2 + (hop - 1) * 2 + way

    def x_send(cam, hop, way):
        k, ref = x_index(cam, hop, way), x_unit(xi, cam, hop, way)
        send(ref, ref, xs.at[k], xr.at[k], xm)
        if cam == 0:
            send(meta.at[z, xi], meta.at[z, xi], xs.at[10], xr.at[10], xm)

    def x_arrive(cam, hop, way):
        k = x_index(cam, hop, way)
        arrive(x_unit(1 - xi, cam, hop, way), xs.at[k], xr.at[k])
        if cam == 0:
            arrive(meta.at[z, 1 - xi], xs.at[10], xr.at[10])

    def z_arrive(stream, hop):
        for way in range(2):
            zz = at(-hop if way == 0 else hop)
            arrive(unit(stream, zz, way if hop == 4 else None), zs.at[way, stream, hop - 1], zr.at[way, stream, hop - 1])
            if noted(stream, way, hop):
                arrive(note(stream, zz), ms.at[way, stream, hop - 1], mr.at[way, stream, hop - 1])
            if hop < 4:
                z_send(stream, way, hop + 1)
            if stream == 2:
                x_send(1, hop, way)

    def embed(cam):
        rows = fv[cam].astype(jnp.float32) * sc[...].reshape(1, FEAT) + sh[...].reshape(1, FEAT)
        normed[...] = rows.astype(jnp.bfloat16)
        projected = jnp.dot(normed[...], pv[...], preferred_element_type=jnp.float32)
        total = jnp.sum(projected * projected, axis=-1, keepdims=True)
        unit_rows = (projected * lax.rsqrt(total + 1e-06)).astype(jnp.bfloat16)
        emb[0, cam] = unit_rows.T

    def emb_send(grp, cam):
        k, to = {2: (0, pm), 1: (1, sib)}[grp]
        send(emb.at[0, cam], emb.at[grp, cam], es.at[k, cam], er.at[k, cam], to)

    def emb_arrive(grp, cam):
        k = {2: 0, 1: 1, 3: 2}[grp]
        arrive(emb.at[grp, cam], es.at[k, cam], er.at[k, cam])
        if grp == 2:
            send(emb.at[2, cam], emb.at[3, cam], es.at[2, cam], er.at[2, cam], sib)

    def score(zz, grp, cam):
        sims = jnp.dot(
            gal[zz].reshape(4 * KEPT, EMB), emb[grp, cam], preferred_element_type=jnp.float32
        )
        frame = lax.broadcasted_iota(jnp.int32, (HALF, CROPS), 0)
        rows = []
        for q in range(4):
            cut = meta[zz, q // 2, pl.ds(q % 2, 1), :]
            full = meta[zz, q // 2, pl.ds(2 + q % 2, 1), :]
            cut = jnp.concatenate([cut, cut], axis=1)
            full = jnp.concatenate([full, full], axis=1)
            whole = sims[q * KEPT : q * KEPT + HALF]
            mixed = sims[q * KEPT + HALF : (q + 1) * KEPT]
            mine = frame < cut
            a = jnp.max(whole, axis=0, keepdims=True)
            u = jnp.max(jnp.where(mine, mixed, -jnp.inf), axis=0, keepdims=True)
            v = jnp.max(jnp.where(mine, -jnp.inf, mixed), axis=0, keepdims=True)
            rows.append(jnp.where(full == 0, a, u))
            rows.append(jnp.where(full == 1, a, jnp.where(full == 0, u, v)))
            rows.append(jnp.where(full == 2, a, v))
        rows.append(jnp.zeros((4, CROPS), jnp.float32))
        return jnp.concatenate(rows, axis=0)

    def work(places, grps, cams):
        ng, nc = grps[1] - grps[0], cams[1] - cams[0]

        def body(t, carry):
            i = places[0] + t // (ng * nc)
            grp, cam = grps[0] + (t // nc) % ng, cams[0] + t % nc
            d = jnp.where(i % 2 == 1, (i + 1) // 2, 0 - i // 2)
            res[grp, i, cam] = score(at(d), grp, cam)
            return carry

        count = (places[1] - places[0]) * ng * nc
        lax.fori_loop(0, count, body, 0, unroll=min(count, 4))

    def give_sib(k):
        lo, n = SIB_PARTS[k]
        send(res.at[1, pl.ds(lo, n)], rsr.at[pl.ds(lo, n)], ss.at[k], sr.at[k], sib)

    def give_pair(m):
        for t, to in enumerate((pm, pmo)):
            rows = [res[2 + t, i, cam][0:ROWS] for i, cam in MESSAGES[m]]
            rps[t, m] = jnp.concatenate(rows, axis=0).astype(jnp.bfloat16)
            send(rps.at[t, m], rpr.at[t, m], ps.at[t, m], pr.at[t, m], to)

    x_send(0, 0, 0)
    z_send(2, 0, 1)
    z_send(2, 1, 1)
    local[2].wait()
    local[3].wait()
    local[4].wait()
    local[5].wait()
    embed(0)
    emb_send(2, 0)
    z_send(0, 0, 1)
    z_send(0, 1, 1)
    x_send(1, 0, 0)
    emb_send(1, 0)
    local[6].wait()
    embed(1)
    emb_send(1, 1)
    x_arrive(0, 0, 0)
    z_send(1, 0, 1)
    z_send(1, 1, 1)

    local[7].wait()
    n_row = lax.broadcasted_iota(jnp.int32, (NEIGH * TRACKS, NEIGH), 0)
    n_col = lax.broadcasted_iota(jnp.int32, (NEIGH * TRACKS, NEIGH), 1) * TRACKS
    same = (n_row >= n_col) & (n_row < n_col + TRACKS)
    for cam in range(CAMS):
        spread = jnp.where(same, av[pl.ds(cam, 1), :].astype(jnp.float32), 0.0).astype(jnp.bfloat16)
        adjc[cam] = jnp.dot(spread, jnp.ones((NEIGH, 128), jnp.bfloat16), preferred_element_type=jnp.float32)

    own, other, all_cams, pair = (0, 1), (1, 2), (0, 2), (2, 4)
    z_arrive(2, 1)
    emb_send(2, 1)
    z_arrive(0, 1)
    x_arrive(1, 0, 0)
    emb_arrive(1, 0)
    emb_arrive(1, 1)
    work((0, 1), (0, 2), all_cams)
    z_arrive(1, 1)
    z_arrive(2, 2)
    x_arrive(1, 1, 0)
    x_arrive(1, 1, 1)
    work((1, 3), own, all_cams)
    z_arrive(0, 2)
    work((1, 3), other, all_cams)
    emb_arrive(2, 0)
    z_arrive(1, 2)
    z_arrive(2, 3)
    emb_arrive(3, 0)
    work((0, 3), pair, (0, 1))
    x_arrive(1, 2, 0)
    x_arrive(1, 2, 1)
    work((3, 4), pair, (0, 1))
    give_pair(0)
    z_arrive(0, 3)
    work((3, 5), own, all_cams)
    work((4, 5), pair, (0, 1))
    emb_arrive(2, 1)
    z_arrive(1, 3)
    work((3, 5), other, all_cams)
    give_sib(0)
    z_arrive(2, 4)
    emb_arrive(3, 1)
    work((0, 4), pair, (1, 2))
    give_pair(1)
    x_arrive(1, 3, 0)
    x_arrive(1, 3, 1)
    work((4, 5), pair, (1, 2))
    work((5, 6), pair, all_cams)
    give_pair(2)
    z_arrive(0, 4)
    work((6, 7), pair, all_cams)
    work((5, 7), (0, 2), all_cams)
    give_sib(1)
    drain(20)
    z_arrive(1, 4)
    x_arrive(1, 4, 0)
    x_arrive(1, 4, 1)
    work((7, 8), pair, all_cams)
    give_pair(3)
    work((7, 8), other, all_cams)
    give_sib(2)
    work((7, 8), own, all_cams)
    drain(6)

    def weave(even, odd):
        return jnp.concatenate([even[0:6], odd[0:6], even[6:12], odd[6:12]], axis=0)

    written = []

    def finish(i):
        zz = at(DELTA[i])
        for cam in range(CAMS):
            m, j = PLACE[i, cam]
            for side in range(2):
                if side == 0:
                    here, there = res[0, i, cam], rsr[i, cam]
                else:
                    here, there = [rpr[t, m, j * ROWS : (j + 1) * ROWS].astype(jnp.float32) for t in range(2)]
                block = weave(jnp.where(c == 0, here, there), jnp.where(c == 0, there, here))
                cls = x // 2 if side == 0 else 1 - x // 2
                at_row = pl.multiple_of(zz * 48 + cls * 24, 8)
                factor = adjc[cam, pl.ds(at_row, 24), :]
                outv[cam, pl.ds(at_row, 24), :] = block * jnp.concatenate([factor, factor], axis=1)
        rows = pl.ds(pl.multiple_of(zz * 48, 8), 48)
        for cam in range(CAMS):
            cp = pltpu.make_async_copy(outv.at[cam, rows], out.at[cam, rows], osem.at[i, cam])
            cp.start()
            written.append(cp)

    def pair_arrive(m):
        for t in range(2):
            arrive(rpr.at[t, m], ps.at[t, m], pr.at[t, m])

    def sib_arrive(k):
        lo, n = SIB_PARTS[k]
        arrive(rsr.at[pl.ds(lo, n)], ss.at[k], sr.at[k])

    sib_arrive(0)
    pair_arrive(0)
    pair_arrive(1)
    for i in range(4):
        finish(i)
    sib_arrive(1)
    pair_arrive(2)
    for i in (4, 5):
        finish(i)
    sib_arrive(2)
    pair_arrive(3)
    for i in (6, 7):
        finish(i)
    drain(0)
    for cp in written:
        cp.wait()


def per_device(feat, counts, scale, shift, proj, gall, fill, adj):
    hbm = pl.BlockSpec(memory_space=pltpu.HBM)
    bf, f32, dma = jnp.bfloat16, jnp.float32, pltpu.SemaphoreType.DMA
    scores = pl.pallas_call(
        kernel,
        name="match",
        out_shape=jax.ShapeDtypeStruct((CAMS, NEIGH * TRACKS, CROPS), f32),
        in_specs=[hbm] * 7,
        out_specs=hbm,
        scratch_shapes=[
            pltpu.SMEM((CAMS, TRACKS), jnp.int32),
            pltpu.VMEM((CAMS, CROPS, FEAT), bf),
            pltpu.VMEM((FEAT, EMB), bf),
            pltpu.VMEM((CAMS, TRACKS, FRAMES, EMB), bf),
            pltpu.VMEM((FEAT,), f32),
            pltpu.VMEM((FEAT,), f32),
            pltpu.VMEM((CAMS, NEIGH), jnp.int32),
            pltpu.VMEM((CAMS, NEIGH * TRACKS, 128), f32),
            pltpu.VMEM((CROPS, FEAT), bf),
            pltpu.VMEM((NZ, 2, CAMS, KEPT, EMB), bf),
            pltpu.VMEM((NZ, 2, 8, 128), jnp.int32),
            pltpu.VMEM((4, CAMS, EMB, CROPS), bf),
            pltpu.VMEM((4, NZ, CAMS, 16, CROPS), f32),
            pltpu.VMEM((NZ, CAMS, 16, CROPS), f32),
            pltpu.VMEM((2, 4, 4 * ROWS, CROPS), bf),
            pltpu.VMEM((2, 4, 4 * ROWS, CROPS), bf),
            pltpu.VMEM((CAMS, NEIGH * TRACKS, CROPS), f32),
            dma((8,)),
            dma((2, 3, 4)),
            dma((2, 3, 4)),
            dma((2, 2, 4)),
            dma((2, 2, 4)),
            dma((11,)),
            dma((11,)),
            dma((3, CAMS)),
            dma((3, CAMS)),
            dma((3,)),
            dma((3,)),
            dma((2, 4)),
            dma((2, 4)),
            dma((NZ, CAMS)),
        ],
        compiler_params=pltpu.CompilerParams(
            collective_id=0, has_side_effects=True, vmem_limit_bytes=60 * 2**20
        ),
    )(feat, scale, shift, proj, gall, fill, adj)
    live = jnp.arange(CROPS, dtype=jnp.int32)[None, :] < counts[:, None]
    return jnp.where(live[:, None, :], scores, 0.0)


def solution(mesh):
    return jax.shard_map(
        per_device,
        mesh=mesh,
        in_specs=(
            P(("region", "stream"), None, None),
            P(("region", "stream")),
            P(),
            P(),
            P(),
            P(("region", "stream"), None, None, None),
            P(("region", "stream"), None),
            P(("region", "stream"), None),
        ),
        out_specs=P(("region", "stream"), None, None),
        check_vma=False,
    )
```

time: 49.8 us -> 37.2 us (0.75)
  local copies, waits for them, and re-layouts: 8.39 us -> 0 us
  Pallas kernels: 41.1 us -> 34.3 us
  other arithmetic: 0 us -> 2.79 us
    unnamed x17 -> x0, local copies, waits for them, and re-layouts: 8.39 us -> none
    pallas_call x1, Pallas kernels: 41.1 us -> 34.3 us  [per_device(): pl.pallas_call(kernel, name='match', out_shape=jax.ShapeDtypeStruct((CAMS...]
    select_n x0 -> x1, other arithmetic: none -> 2.07 us  [per_device(): return jnp.where(live[:, None, :], scores, 0.0)]
    lt x0 -> x1, other arithmetic: none -> 0.73 us  [per_device(): live = jnp.arange(CROPS, dtype=jnp.int32)[None, :] < counts[:, None]]
where the time goes in v2:
time: 37.2 us; the launch traced here: 37.1 us
  Pallas kernels  34.3 us (92%)
  other arithmetic  2.79 us (7%)
    pallas_call x1, Pallas kernels, per_device(): pl.pallas_call(kernel, name='match', out_shape=jax.ShapeDtypeStruct((CAMS...  34.3 us
    select_n x1, other arithmetic, per_device(): return jnp.where(live[:, None, :], scores, 0.0)  2.07 us

profile of v2, /device:TPU:1, one launch (start us, length us, event | category | flops | bytes accessed | tf_op | source)
XLA Modules:
  0.0 37.1 jit_solution(8696068087155478841)
XLA Ops:
  0.0 0.7 %iota_compare_fusion = pred[2,256]{1,0:T(4,128)(4,1)S(1)} fusion(s32[2]{0:T(128)} %param.9), kind=kLoop, calls=%fused_computation.1 | loop fusion | flops 512 | bytes 520 | tf_op jit(solution)/shard_map/lt | solution.py:400
  0.7 34.3 %match.1 = f32[2,384,256]{2,1,0:T(8,128)} custom-call(bf16[2,256,2048]{2,1,0:T(8,128)(2,1)} %feat.1, f32[2048]{0:T(1024)} %scale.1, f32[2048]{0:T(1024)} %shift.1, bf16[2048,512]{1,0:T(8,128)(2,1)} %proj.1, bf16[2,3,32,512]{3,2,1,0:T(8,128)(2,1)} %gall.1, s32[2,3]{1,0:T(2,128)} %fill_in.1, s32[2,128]{1,0:T(2,128)} %adj.1), custom_call_target="tpu_custom_call" | custom-call | tf_op jit(solution)/shard_map/match/pallas_call | solution.py:357
  35.0 2.1 %broadcast_select_fusion = f32[2,384,256]{2,1,0:T(8,128)} fusion(f32[2,384,256]{2,1,0:T(8,128)} %match.1, pred[2,256]{1,0:T(4,128)(4,1)S(1)} %iota_compare_fusion), kind=kLoop, calls=%fused_computation | loop fusion | flops 196608 | bytes 1573376 | tf_op jit(solution)/shard_map/jit(_where)/select_n | solution.py:401

commit v3 on v2

--- a/solution.py
+++ b/solution.py
@@ -23,9 +23,9 @@
 
 
 def kernel(
-    feat, scale, shift, proj, gall, fill_in, adj, out,
-    fill, fv, pv, gv, sc, sh, av, adjc, normed, gal, meta, emb, res, rsr, rps, rpr, outv,
-    lsem, zs, zr, ms, mr, xs, xr, es, er, ss, sr, ps, pr, osem,
+    feat, counts_in, scale, shift, proj, gall, fill_in, adj, out,
+    counts, fill, fv, pv, gv, sc, sh, av, adjc, normed, gal, meta, emb, res, rsr, rps, rpr,
+    lsem, zs, zr, ms, mr, xs, xr, es, er, ss, sr, ps, pr,
 ):
     r, s = lax.axis_index("region"), lax.axis_index("stream")
     z, x, c = r // 8, (r // 2) % 4, r % 2
@@ -53,6 +53,7 @@
         pltpu.make_async_copy(feat.at[0], fv.at[0], lsem.at[4]),
         pltpu.make_async_copy(feat.at[1], fv.at[1], lsem.at[5]),
         pltpu.make_async_copy(adj, av, lsem.at[6]),
+        pltpu.make_async_copy(counts_in, counts, lsem.at[8]),
     ]
     for cp in local:
         cp.start()
@@ -238,6 +239,7 @@
     z_send(1, 1, 1)
 
     local[7].wait()
+    local[8].wait()
     n_row = lax.broadcasted_iota(jnp.int32, (NEIGH * TRACKS, NEIGH), 0)
     n_col = lax.broadcasted_iota(jnp.int32, (NEIGH * TRACKS, NEIGH), 1) * TRACKS
     same = (n_row >= n_col) & (n_row < n_col + TRACKS)
@@ -303,7 +305,7 @@
     def weave(even, odd):
         return jnp.concatenate([even[0:6], odd[0:6], even[6:12], odd[6:12]], axis=0)
 
-    written = []
+    lane = lax.broadcasted_iota(jnp.int32, (24, CROPS), 1)
 
     def finish(i):
         zz = at(DELTA[i])
@@ -318,12 +320,8 @@
                 cls = x // 2 if side == 0 else 1 - x // 2
                 at_row = pl.multiple_of(zz * 48 + cls * 24, 8)
                 factor = adjc[cam, pl.ds(at_row, 24), :]
-                outv[cam, pl.ds(at_row, 24), :] = block * jnp.concatenate([factor, factor], axis=1)
-        rows = pl.ds(pl.multiple_of(zz * 48, 8), 48)
-        for cam in range(CAMS):
-            cp = pltpu.make_async_copy(outv.at[cam, rows], out.at[cam, rows], osem.at[i, cam])
-            cp.start()
-            written.append(cp)
+                block = block * jnp.concatenate([factor, factor], axis=1)
+                out[cam, pl.ds(at_row, 24), :] = jnp.where(lane < counts[cam], block, 0.0)
 
     def pair_arrive(m):
         for t in range(2):
@@ -347,20 +345,19 @@
     for i in (6, 7):
         finish(i)
     drain(0)
-    for cp in written:
-        cp.wait()
 
 
 def per_device(feat, counts, scale, shift, proj, gall, fill, adj):
     hbm = pl.BlockSpec(memory_space=pltpu.HBM)
     bf, f32, dma = jnp.bfloat16, jnp.float32, pltpu.SemaphoreType.DMA
-    scores = pl.pallas_call(
+    return pl.pallas_call(
         kernel,
         name="match",
-        out_shape=jax.ShapeDtypeStruct((CAMS, NEIGH * TRACKS, CROPS), f32),
-        in_specs=[hbm] * 7,
-        out_specs=hbm,
+        out_shape=pltpu.VMEM((CAMS, NEIGH * TRACKS, CROPS), f32),
+        in_specs=[hbm] * 8,
+        out_specs=pl.BlockSpec(memory_space=pltpu.VMEM),
         scratch_shapes=[
+            pltpu.SMEM((CAMS,), jnp.int32),
             pltpu.SMEM((CAMS, TRACKS), jnp.int32),
             pltpu.VMEM((CAMS, CROPS, FEAT), bf),
             pltpu.VMEM((FEAT, EMB), bf),
@@ -377,8 +374,7 @@
             pltpu.VMEM((NZ, CAMS, 16, CROPS), f32),
             pltpu.VMEM((2, 4, 4 * ROWS, CROPS), bf),
             pltpu.VMEM((2, 4, 4 * ROWS, CROPS), bf),
-            pltpu.VMEM((CAMS, NEIGH * TRACKS, CROPS), f32),
-            dma((8,)),
+            dma((9,)),
             dma((2, 3, 4)),
             dma((2, 3, 4)),
             dma((2, 2, 4)),
@@ -391,14 +387,11 @@
             dma((3,)),
             dma((2, 4)),
             dma((2, 4)),
-            dma((NZ, CAMS)),
         ],
         compiler_params=pltpu.CompilerParams(
             collective_id=0, has_side_effects=True, vmem_limit_bytes=60 * 2**20
         ),
-    )(feat, scale, shift, proj, gall, fill, adj)
-    live = jnp.arange(CROPS, dtype=jnp.int32)[None, :] < counts[:, None]
-    return jnp.where(live[:, None, :], scores, 0.0)
+    )(feat, counts, scale, shift, proj, gall, fill, adj)
 
 
 def solution(mesh):

time: 37.2 us -> 34.5 us (0.927)
  other arithmetic: 2.79 us -> 0 us
  local copies, waits for them, and re-layouts: 0 us -> 0.88 us
  Pallas kernels: 34.3 us -> 33.5 us
    select_n x1 -> x0, other arithmetic: 2.07 us -> none  [per_device(): return jnp.where(live[:, None, :], scores, 0.0)]
    unnamed x0 -> x1, local copies, waits for them, and re-layouts: none -> 0.88 us
    pallas_call x1, Pallas kernels: 34.3 us -> 33.5 us  [per_device(): pl.pallas_call(kernel, name='match', out_shape=pltpu.VMEM((CAMS, NEIGH *...]
    lt x1 -> x0, other arithmetic: 0.73 us -> none  [per_device(): live = jnp.arange(CROPS, dtype=jnp.int32)[None, :] < counts[:, None]]
where the time goes in v3:
time: 34.5 us; the launch traced here: 34.4 us
  Pallas kernels  33.5 us (97%)
  local copies, waits for them, and re-layouts  0.88 us (3%)
    pallas_call x1, Pallas kernels, per_device(): pl.pallas_call(kernel, name='match', out_shape=pltpu.VMEM((CAMS, NEIGH *...  33.5 us
    unnamed x1, local copies, waits for them, and re-layouts  0.88 us

profile of v3, /device:TPU:1, one launch (start us, length us, event | category | flops | bytes accessed | tf_op | source)
XLA Modules:
  0.0 34.4 jit_solution(17964604003973995372)
XLA Ops:
  0.0 33.5 %match.1 = f32[2,384,256]{2,1,0:T(8,128)S(1)} custom-call(bf16[2,256,2048]{2,1,0:T(8,128)(2,1)} %feat.1, s32[2]{0:T(128)} %counts_in.1, f32[2048]{0:T(1024)} %scale.1, f32[2048]{0:T(1024)} %shift.1, bf16[2048,512]{1,0:T(8,128)(2,1)} %proj.1, bf16[2,3,32,512]{3,2,1,0:T(8,128)(2,1)} %gall.1, s32[2,3]{1,0:T(2,128)} %fill_in.1, s32[2,128]{1,0:T(2,128)} %adj.1), custom_call_target="tpu_custom_call" | custom-call | tf_op jit(solution)/shard_map/match/pallas_call | solution.py:353
  33.5 0.9 %copy.10 = f32[2,384,256]{2,1,0:T(8,128)} copy(f32[2,384,256]{2,1,0:T(8,128)S(1)} %match.1) | data formatting | bytes 1572864

commit v4 on v3

--- a/solution.py
+++ b/solution.py
@@ -55,12 +55,14 @@
         pltpu.make_async_copy(adj, av, lsem.at[6]),
         pltpu.make_async_copy(counts_in, counts, lsem.at[8]),
     ]
-    for cp in local:
+    for cp in local[:2]:
         cp.start()
     barrier = pltpu.get_barrier_semaphore()
     peers = (sib, xm, pm, pmo, zp, zn)
     for t in peers:
         pl.semaphore_signal(barrier, inc=1, device_id=t, device_id_type=MESH)
+    for cp in local[2:]:
+        cp.start()
 
     local[0].wait()
     local[1].wait()
@@ -111,10 +113,10 @@
         return ref if part is None else ref.at[pl.ds(part * HALF, HALF)]
 
     def note(stream, zz):
-        return meta.at[zz, 1 - xi if stream == 1 else xi]
+        return meta.at[zz]
 
     def noted(stream, way, hop):
-        return stream < 2 and not (way == 1 and hop == 4)
+        return stream == 1 and not (way == 1 and hop == 4)
 
     def z_send(stream, way, hop):
         ref = unit(stream, at(-(hop - 1) if way == 0 else hop - 1), way if hop == 4 else None)
@@ -122,7 +124,7 @@
         send(ref, ref, zs.at[way, stream, hop - 1], zr.at[way, stream, hop - 1], to)
         if noted(stream, way, hop):
             ref = note(stream, at(-(hop - 1) if way == 0 else hop - 1))
-            send(ref, ref, ms.at[way, stream, hop - 1], mr.at[way, stream, hop - 1], to)
+            send(ref, ref, ms.at[way, hop - 1], mr.at[way, hop - 1], to)
 
     def x_unit(column, cam, hop, way):
         ref = gal.at[at(-hop if way == 0 else hop), column, cam]
@@ -148,7 +150,7 @@
             zz = at(-hop if way == 0 else hop)
             arrive(unit(stream, zz, way if hop == 4 else None), zs.at[way, stream, hop - 1], zr.at[way, stream, hop - 1])
             if noted(stream, way, hop):
-                arrive(note(stream, zz), ms.at[way, stream, hop - 1], mr.at[way, stream, hop - 1])
+                arrive(note(stream, zz), ms.at[way, hop - 1], mr.at[way, hop - 1])
             if hop < 4:
                 z_send(stream, way, hop + 1)
             if stream == 2:
@@ -307,11 +309,11 @@
 
     lane = lax.broadcasted_iota(jnp.int32, (24, CROPS), 1)
 
-    def finish(i):
+    def finish(i, sides=(0, 1)):
         zz = at(DELTA[i])
         for cam in range(CAMS):
             m, j = PLACE[i, cam]
-            for side in range(2):
+            for side in sides:
                 if side == 0:
                     here, there = res[0, i, cam], rsr[i, cam]
                 else:
@@ -341,9 +343,12 @@
     for i in (4, 5):
         finish(i)
     sib_arrive(2)
+    for i in (6, 7):
+        finish(i, (0,))
+    drain(2)
     pair_arrive(3)
     for i in (6, 7):
-        finish(i)
+        finish(i, (1,))
     drain(0)
 
 
@@ -377,8 +382,8 @@
             dma((9,)),
             dma((2, 3, 4)),
             dma((2, 3, 4)),
-            dma((2, 2, 4)),
-            dma((2, 2, 4)),
+            dma((2, 4)),
+            dma((2, 4)),
             dma((11,)),
             dma((11,)),
             dma((3, CAMS)),

time: 34.5 us -> 34.2 us (level)
  no operation moved by 1% of the time
where the time goes in v4:
time: 34.2 us; the launch traced here: 34.1 us
  Pallas kernels  33.3 us (97%)
  local copies, waits for them, and re-layouts  0.88 us (3%)
    pallas_call x1, Pallas kernels, per_device(): pl.pallas_call(kernel, name='match', out_shape=pltpu.VMEM((CAMS, NEIGH *...  33.3 us
    unnamed x1, local copies, waits for them, and re-layouts  0.88 us

profile of v4, /device:TPU:1, one launch (start us, length us, event | category | flops | bytes accessed | tf_op | source)
XLA Modules:
  0.0 34.1 jit_solution(1235279172312674099)
XLA Ops:
  0.0 33.3 %match.1 = f32[2,384,256]{2,1,0:T(8,128)S(1)} custom-call(bf16[2,256,2048]{2,1,0:T(8,128)(2,1)} %feat.1, s32[2]{0:T(128)} %counts_in.1, f32[2048]{0:T(1024)} %scale.1, f32[2048]{0:T(1024)} %shift.1, bf16[2048,512]{1,0:T(8,128)(2,1)} %proj.1, bf16[2,3,32,512]{3,2,1,0:T(8,128)(2,1)} %gall.1, s32[2,3]{1,0:T(2,128)} %fill_in.1, s32[2,128]{1,0:T(2,128)} %adj.1), custom_call_target="tpu_custom_call" | custom-call | tf_op jit(solution)/shard_map/match/pallas_call | solution.py:358
  33.3 0.9 %copy.10 = f32[2,384,256]{2,1,0:T(8,128)} copy(f32[2,384,256]{2,1,0:T(8,128)S(1)} %match.1) | data formatting | bytes 1572864
